TPU v7x, 512 devices: a whole 4x4x16 slice. The times are simulated.
512 devices in a mesh: row: 16 (over x, z_hi), col: 32 (over y, z_lo, core).
Axes of the slice: x: 4, y: 4, z: 16 (z_hi: 4, z_lo: 4; z = z_hi * 4 + z_lo), core: 2. Of those that a mesh axis runs over, the one named last changes fastest.
Arguments:
- momentum: bfloat16 [3584, 18432], P('row', 'col'), may hold values from -0.0390625 to 0.0390625
Outputs:
- update: bfloat16 [3584, 18432], P('row', 'col')
All inputs are finite; a program needn't handle non-finite values.
Results may differ from a plain program's by a relative error of at most 0.0088.
Values may be sent and summed in bfloat16 or wider, within the bound.
A program may use at most 64 MiB of HBM per device.

v0:
```python
import jax
import jax.numpy as jnp
from jax import lax
from jax.sharding import PartitionSpec as P

NR = 3584
NC = 18432


coef_a = 3.4445
coef_b = -4.775
coef_c = 2.0315


def on_device(momentum):
    slab_panel = lax.all_gather(momentum, "row", axis=0, tiled=True)
    slab_piece = slab_panel
    summed_tile = lax.psum_scatter(
        lax.dot_general(
            slab_piece, momentum, (((1,), (1,)), ((), ())), preferred_element_type=jnp.float32
        ),
        "col",
        scatter_dimension=0,
        tiled=True,
    )
    gram_tile = summed_tile.T.astype(jnp.bfloat16)
    gram_rows = lax.all_gather(gram_tile, "col", axis=1, tiled=True)
    gram_cols = lax.all_gather(gram_tile, "row", axis=0, tiled=True)
    square_tile = jnp.dot(gram_rows, gram_cols, preferred_element_type=jnp.float32)
    poly_tile = (coef_b * gram_tile.astype(jnp.float32) + coef_c * square_tile).astype(jnp.bfloat16)
    slab_piece = slab_panel
    combined = jnp.dot(
        lax.all_gather(poly_tile, "col", axis=1, tiled=True),
        slab_piece,
        preferred_element_type=jnp.float32,
    )
    factor = 0.2 * max(NR, NC) ** 0.5
    return (factor * (coef_a * momentum.astype(jnp.float32) + combined)).astype(jnp.bfloat16)


def solution(mesh):
    in_specs = (P("row", "col"),)
    out_specs = P("row", "col")
    return jax.shard_map(
        on_device, mesh=mesh, in_specs=in_specs, out_specs=out_specs, check_vma=False
    )
```

profile of v0, /device:TPU:1, one launch (start us, length us, event | category | flops | bytes accessed | tf_op | source)
XLA Modules:
  0.0 467.6 jit_solution(16442331392117206114)
XLA Ops:
  6.5 0.0 all-gather.4.cloned.1.call-start
  6.5 0.7 all-gather.4.cloned.1.call-update
  7.3 0.0 reduce-scatter.2.cloned.1.call-start
  7.3 149.4 %all-gather.4.cloned.1.call-done = bf16[3584,576]{1,0:T(8,128)(2,1)} async-done(((bf16[224,576]{1,0:T(8,128)(2,1)}), bf16[3584,576]{1,0:T(8,128)(2,1)}) %all-gather.4.cloned.1.call-update) | async-done | bytes 4128784 | tf_op jit(solution)/shard_map/all_gather | solution.py:16
  156.7 5.8 %fusion.4 = f32[3584,224]{1,0:T(8,128)} fusion(bf16[3584,576]{1,0:T(8,128)(2,1)} %all-gather.4.cloned.1.call-done, bf16[224,576]{1,0:T(8,128)(2,1)} %param.1), kind=kOutput, calls=%fused_computation.7 | convolution fusion | flops 924844032 | bytes 7598080 | tf_op jit(solution)/shard_map/dot_general | solution.py:19
  162.5 0.0 copy-start
  162.5 0.0 reduce-scatter.2.cloned.1.call-update
  162.5 0.0 all-gather.6.cloned.1.call-start
  162.5 149.2 %reduce-scatter.2.cloned.1.call-done = f32[112,224]{1,0:T(8,128)} async-done(((f32[3584,224]{1,0:T(8,128)}), f32[112,224]{1,0:T(8,128)}) %reduce-scatter.2.cloned.1.call-update) | async-done | bytes 100368 | tf_op jit(solution)/shard_map/reduce_scatter | solution.py:18
  311.7 1.5 convert_bitcast_fusion
  313.2 0.0 all-gather.6.cloned.1.call-update
  313.3 0.0 all-gather.8.cloned.1.call-start
  313.3 0.9 copy.2
  314.2 65.1 %all_gather.14 = bf16[3584,112]{1,0:T(8,128)(2,1)S(1)} all-gather(bf16[224,112]{1,0:T(8,128)(2,1)S(1)} %copy.2), channel_id=1, replica_groups=mesh['row'=16,'col'=32] {'row'}, dimensions={0}, use_global_device_ids=true | all-gather | bytes 852992 | tf_op jit(solution)/shard_map/all_gather | solution.py:28
  379.3 11.6 %all-gather.6.cloned.1.call-done = bf16[224,3584]{0,1:T(8,128)(2,1)} async-done(((bf16[224,112]{0,1:T(8,128)(2,1)}), bf16[224,3584]{0,1:T(8,128)(2,1)}) %all-gather.6.cloned.1.call-update) | async-done | bytes 1605648 | tf_op jit(solution)/shard_map/all_gather | solution.py:27
  391.0 2.7 fusion.3
  393.6 0.0 all-gather.8.cloned.1.call-update
  393.7 62.4 %all-gather.8.cloned.1.call-done = bf16[224,3584]{0,1:T(8,128)(2,1)} async-done(((bf16[224,112]{0,1:T(8,128)(2,1)}), bf16[224,3584]{0,1:T(8,128)(2,1)}) %all-gather.8.cloned.1.call-update) | async-done | bytes 1605648 | tf_op jit(solution)/shard_map/all_gather | solution.py:33
  456.1 0.0 copy-done
  456.1 5.0 %fusion.1 = bf16[224,576]{1,0:T(8,128)(2,1)} fusion(bf16[224,3584]{0,1:T(8,128)(2,1)} %all-gather.8.cloned.1.call-done, bf16[3584,576]{1,0:T(8,128)(2,1)} %all-gather.4.cloned.1.call-done, bf16[224,576]{1,0:T(8,128)(2,1)S(1)} %copy-done), kind=kOutput, calls=%fused_computation.2 | convolution fusion | flops 925489152 | bytes 6250496 | tf_op jit(solution)/shard_map/dot_general | solution.py:32
Async XLA Ops:
  6.5 150.2 %all-gather.4.cloned.1.call-start = ((), (), s32[]{:S(2)}) async-start(), calls=%async_computation.1 | async-start | bytes 4874240 | tf_op jit(solution)/shard_map/all_gather | solution.py:16
  7.3 304.5 %reduce-scatter.2.cloned.1.call-start = ((), (), s32[]{:S(2)}) async-start(), calls=%async_computation.2 | async-start | bytes 3784704 | tf_op jit(solution)/shard_map/reduce_scatter | solution.py:18
  162.5 293.6 %copy-start = (bf16[224,576]{1,0:T(8,128)(2,1)S(1)}, bf16[224,576]{1,0:T(8,128)(2,1)}, u32[]{:S(2)}) copy-start(bf16[224,576]{1,0:T(8,128)(2,1)} %param.1) | copy-start | bytes 774148
  162.5 228.5 %all-gather.6.cloned.1.call-start = ((), (), s32[]{:S(2)}) async-start(), calls=%async_computation.3 | async-start | bytes 1892352 | tf_op jit(solution)/shard_map/all_gather | solution.py:27
  313.3 142.8 %all-gather.8.cloned.1.call-start = ((), (), s32[]{:S(2)}) async-start(), calls=%async_computation.4 | async-start | bytes 1892352 | tf_op jit(solution)/shard_map/all_gather | solution.py:33
Sparse Core Ops, SparseCore 0:
  10.4 146.2 all-gather.3
  162.6 149.0 reduce-scatter.1
  314.1 76.8 all-gather.5
  393.8 62.2 all-gather.7
where the time goes:
time: 468 us
  waiting for transfers between devices  373 us (80%)
  blocking collectives  65.1 us (14%)
  matrix products  13.5 us (3%)
  between operations  13.1 us (3%)
    all_gather x1, waiting for transfers between devices, on_device(): slab_panel = lax.all_gather(momentum, 'row', axis=0, tiled=True)  149 us
    reduce_scatter x1, waiting for transfers between devices, on_device(): lax.psum_scatter(lax.dot_general(slab_piece, momentum, (((1,), (1,)), (()...  149 us
    all_gather x1, blocking collectives, on_device(): gram_cols = lax.all_gather(gram_tile, 'row', axis=0, tiled=True)  65.1 us
    all_gather x1, waiting for transfers between devices, on_device(): lax.all_gather(poly_tile, 'col', axis=1, tiled=True)  62.4 us
    all_gather x1, waiting for transfers between devices, on_device(): gram_rows = lax.all_gather(gram_tile, 'col', axis=1, tiled=True)  11.6 us
  transfers between devices with their start and end apart: 4, of which 4 were waited for; matrix products, arithmetic and copies ran while one was open for 0% of the time, Pallas kernels for 0%

commit v1 on v0

v1 whole, which is shorter than its diff:
```python
import jax
import jax.numpy as jnp
from jax import lax
from jax.experimental import pallas as pl
from jax.experimental.pallas import tpu as pltpu
from jax.sharding import PartitionSpec as P

NR = 3584
NC = 18432

coef_a = 3.4445
coef_b = -4.775
coef_c = 2.0315
factor = 0.2 * max(NR, NC) ** 0.5

MESH = pl.DeviceIdType.MESH

B = 224
H = 112
W = 576
TILES = 4
PACK = TILES * B + H
CUTS = ((0, 256), (256, 256), (512, 256), (768, 240))
UP = (0, 1)
DOWN = (2, 3)


def nt_dot(a, b):
    return lax.dot_general(a, b, (((1,), (1,)), ((), ())), preferred_element_type=jnp.float32)


def nn_dot(a, b):
    return lax.dot_general(a, b, (((1,), (0,)), ((), ())), preferred_element_type=jnp.float32)


def kernel(
    x_ref,
    o_ref,
    xs,
    part,
    send1,
    recv1,
    send2,
    recv2,
    sum2,
    send3,
    recv3,
    gr,
    gc,
    pr,
    acc,
    xsend,
    xrecv,
    rsend,
    rrecv,
    gsend,
    grecv,
    psend,
    precv,
):
    row = lax.axis_index("row")
    col = lax.axis_index("col")
    x, zh = row // 4, row % 4
    y, zl, k = col // 8, (col // 2) % 4, col % 2

    def at(dx=0, dzh=0, dy=0, dzl=0, dk=0):
        return (
            ((x + dx) % 4) * 4 + (zh + dzh) % 4,
            ((y + dy) % 4) * 8 + ((zl + dzl) % 4) * 2 + (k + dk) % 2,
        )

    started = []

    def send(src, dst, ssem, rsem, device):
        copy = pltpu.make_async_remote_copy(
            src_ref=src, dst_ref=dst, send_sem=ssem, recv_sem=rsem, device_id=device, device_id_type=MESH
        )
        copy.start()
        started.append(copy)

    def arrived(dst, rsem):
        pltpu.make_async_copy(dst, dst, rsem).wait()

    def unpack(zp, xp):
        tiles = [xs[zp, xp, pl.ds(t * B, B), :] for t in range(TILES)]
        last = xs[zp, xp, pl.ds(TILES * B, H), :]
        tiles.append(jnp.concatenate([last[:, :64], last[:, 64:]], axis=0))
        return jnp.concatenate(tiles, axis=1)

    for t in range(TILES):
        xs[zh, x, pl.ds(t * B, B), :] = x_ref[:, pl.ds(t * 128, 128)]
    xs[zh, x, pl.ds(TILES * B, H), :] = jnp.concatenate(
        [x_ref[pl.ds(0, H), pl.ds(TILES * 128, 64)], x_ref[pl.ds(H, H), pl.ds(TILES * 128, 64)]], axis=1
    )

    barrier = pltpu.get_barrier_semaphore()
    peers = [at(dx=d) for d in (1, 2, 3)] + [at(dzh=d) for d in (1, 2, 3)]
    peers += [at(dy=d) for d in (1, 2, 3)] + [at(dzl=d) for d in (1, 2, 3)] + [at(dk=1)]
    for peer in peers:
        pl.semaphore_signal(barrier, 1, device_id=peer, device_id_type=MESH)
    pl.semaphore_wait(barrier, len(peers))

    def xpiece(dz, dx, ch):
        start, size = CUTS[ch]
        return xs.at[(zh + dz) % 4, (x + dx) % 4, pl.ds(start, size)]

    def xmove(kind, dz, dx, ch, hop_z, hop_x):
        there = ((dz - hop_z) % 4, (dx - hop_x) % 4)
        piece = xpiece(dz, dx, ch)
        send(piece, piece, xsend.at[kind, dz, ch], xrecv.at[there[0], there[1], ch], at(dx=hop_x, dzh=hop_z))

    def xwait(dz, dx, ch):
        arrived(xpiece(dz, dx, ch), xrecv.at[dz, dx, ch])

    def x_spread(dz, ch):
        xmove(0, dz, 0, ch, 0, 1)
        xmove(1, dz, 0, ch, 0, 3)

    def x_forward(dz, ch):
        if ch in UP:
            xwait(dz, 3, ch)
            xmove(2, dz, 3, ch, 0, 1)
        else:
            xwait(dz, 1, ch)
            xmove(2, dz, 1, ch, 0, 3)

    def x_rest(dz):
        for ch in range(4):
            xwait(dz, 1 if ch in UP else 3, ch)
            xwait(dz, 2, ch)

    def z_forward(ch):
        if ch in UP:
            xwait(3, 0, ch)
            xmove(4, 3, 0, ch, 1, 0)
            x_spread(3, ch)
        else:
            xwait(1, 0, ch)
            xmove(4, 1, 0, ch, 3, 0)
            x_spread(1, ch)

    def z_last(ch):
        dz = 1 if ch in UP else 3
        xwait(dz, 0, ch)
        x_spread(dz, ch)

    def gram(dz):
        zp = (zh + dz) % 4

        def step(xp, carry):
            part[dz, xp] = nt_dot(x_ref[...], unpack(zp, xp))
            send1[dz, xp] = part[dz, xp, pl.ds((1 - k) * H, H), :].astype(jnp.bfloat16)
            return carry

        lax.fori_loop(0, 4, step, 0)
        send(send1.at[dz], recv1.at[dz], rsend.at[0, dz], rrecv.at[0, dz], at(dk=1))

    def reduce_core(dz):
        arrived(recv1.at[dz], rrecv.at[0, dz])

        def both(xp):
            return part[dz, xp, pl.ds(k * H, H), :] + recv1[dz, xp].astype(jnp.float32)

        for dy in (1, 2, 3):
            send2[dz, dy - 1] = both((y + dy) % 4).astype(jnp.bfloat16)
            send(send2.at[dz, dy - 1], recv2.at[dz, dy - 1], rsend.at[dy, dz], rrecv.at[dy, dz], at(dy=dy))
        sum2[dz] = both(y)

    def reduce_y(dz):
        for dy in (1, 2, 3):
            arrived(recv2.at[dz, dy - 1], rrecv.at[dy, dz])
        total = sum2[dz]
        for dy in (1, 2, 3):
            total = total + recv2[dz, dy - 1].astype(jnp.float32)
        sum2[dz] = total

    for n in range(2):
        xmove(3, 0, 0, UP[n], 1, 0)
        xmove(5, 0, 0, DOWN[n], 3, 0)
        xmove(0, 0, 0, UP[n], 0, 1)
        xmove(1, 0, 0, DOWN[n], 0, 3)
    for n in range(2):
        xmove(3, 0, 0, DOWN[n], 1, 0)
        xmove(5, 0, 0, UP[n], 3, 0)
        xmove(0, 0, 0, DOWN[n], 0, 1)
        xmove(1, 0, 0, UP[n], 0, 3)
    for n in range(2):
        x_forward(0, UP[n])
        x_forward(0, DOWN[n])
    z_forward(UP[0])
    z_forward(DOWN[0])
    x_rest(0)
    gram(0)
    z_forward(UP[1])
    z_forward(DOWN[1])
    reduce_core(0)
    x_forward(3, UP[0])
    x_forward(1, DOWN[0])
    x_forward(3, UP[1])
    x_forward(1, DOWN[1])
    z_last(DOWN[0])
    z_last(UP[0])
    reduce_y(0)
    z_last(DOWN[1])
    z_last(UP[1])
    x_forward(3, DOWN[0])
    x_forward(1, UP[0])
    xwait(2, 0, UP[0])
    x_spread(2, UP[0])
    xwait(2, 0, DOWN[0])
    x_spread(2, DOWN[0])
    x_forward(3, DOWN[1])
    x_forward(1, UP[1])
    x_rest(3)
    gram(3)
    x_rest(1)
    gram(1)
    x_forward(2, UP[0])
    x_forward(2, DOWN[0])
    reduce_core(3)
    reduce_core(1)
    xwait(2, 0, UP[1])
    x_spread(2, UP[1])
    xwait(2, 0, DOWN[1])
    x_spread(2, DOWN[1])
    reduce_y(3)
    reduce_y(1)
    x_forward(2, UP[1])
    x_forward(2, DOWN[1])
    x_rest(2)
    gram(2)
    reduce_core(2)
    reduce_y(2)

    for d in (1, 2, 3):
        send3[d - 1] = sum2[(zl + d - zh + 4) % 4].astype(jnp.bfloat16)
        send(send3.at[d - 1], recv3.at[d - 1], rsend.at[4, d], rrecv.at[4, d], at(dzl=d))
    total = sum2[(zl - zh + 4) % 4]
    for d in (1, 2, 3):
        arrived(recv3.at[d - 1], rrecv.at[4, d])
        total = total + recv3[d - 1].astype(jnp.float32)
    tile = total.astype(jnp.bfloat16)

    gr[zl, y] = tile
    gc[zh, k, x] = tile

    def row_move(buf, ssem, rsem, dzl, hop_zl, hop_y):
        piece = buf((zl + dzl) % 4, y)
        kind = hop_zl if hop_zl else 3 + hop_y
        there = ((dzl - hop_zl) % 4, (0 - hop_y) % 4)
        send(piece, piece, ssem.at[kind, dzl], rsem.at[there[0], there[1]], at(dzl=hop_zl, dy=hop_y))

    def gr_at(zp, yp):
        return gr.at[zp, yp]

    def gc_move(dz, hop_z, hop_x):
        piece = gc.at[(zh + dz) % 4, k, x]
        kind = 7 + (hop_z if hop_z else 3 + hop_x)
        there = ((dz - hop_z) % 4, (0 - hop_x) % 4)
        send(piece, piece, gsend.at[kind, dz], grecv.at[4 + there[0], there[1]], at(dzh=hop_z, dx=hop_x))

    for d in (1, 3, 2):
        gc_move(0, d, 0)
        row_move(gr_at, gsend, grecv, 0, d, 0)
    for d in (1, 3, 2):
        gc_move(0, 0, d)
        row_move(gr_at, gsend, grecv, 0, 0, d)
    for n in (3, 1, 2):
        arrived(gr.at[(zl + n) % 4, y], grecv.at[n, 0])
        for d in (1, 3, 2):
            row_move(gr_at, gsend, grecv, n, 0, d)
    for n in (3, 1, 2):
        arrived(gc.at[(zh + n) % 4, k, x], grecv.at[4 + n, 0])
        for d in (1, 3, 2):
            gc_move(n, 0, d)
    for n in (0, 3, 1, 2):
        zp = (zh + n) % 4
        for d in (1, 3, 2):
            arrived(gc.at[zp, k, (x + d) % 4], grecv.at[4 + n, d])
        send(gc.at[zp, k], gc.at[zp, k], gsend.at[14, n], grecv.at[8, n], at(dk=1))
    for n in range(4):
        for d in (1, 3, 2):
            arrived(gr.at[(zl + n) % 4, (y + d) % 4], grecv.at[n, d])
    for n in range(4):
        zp = (zh + n) % 4
        arrived(gc.at[zp, 1 - k], grecv.at[8, n])

    square = jnp.zeros((H, B), jnp.float32)
    for zp in range(4):
        for xp in range(4):
            right = jnp.concatenate([gc[zp, 0, xp], gc[zp, 1, xp]], axis=0)
            square = square + nn_dot(gr[zp, xp], right)
    pr[zl, k, y] = (coef_b * gr[zl, y].astype(jnp.float32) + coef_c * square).astype(jnp.bfloat16)

    def pr_at(zp, yp):
        return pr.at[zp, k, yp]

    for d in (1, 3, 2):
        row_move(pr_at, psend, precv, 0, d, 0)
    for d in (1, 3, 2):
        row_move(pr_at, psend, precv, 0, 0, d)
    for n in (3, 1, 2):
        arrived(pr_at((zl + n) % 4, y), precv.at[n, 0])
        for d in (1, 3, 2):
            row_move(pr_at, psend, precv, n, 0, d)
    for n in (0, 3, 1, 2):
        zp = (zl + n) % 4
        for d in (1, 3, 2):
            arrived(pr_at(zp, (y + d) % 4), precv.at[n, d])
        send(pr.at[zp, k], pr.at[zp, k], psend.at[7, n], precv.at[4, n], at(dk=1))

    for n, d in enumerate((0, 3, 1, 2)):
        zp = (zl + d) % 4
        arrived(pr.at[zp, 1 - k], precv.at[4, d])

        def step(xp, carry, zp=zp, first=n == 0):
            left = jnp.concatenate([pr[zp, 0, xp], pr[zp, 1, xp]], axis=0)
            acc[...] += nn_dot(left, unpack(zp, xp))
            return carry

        if n == 0:
            acc[...] = coef_a * x_ref[...].astype(jnp.float32)
        lax.fori_loop(0, 4, step, 0)
    o_ref[...] = (factor * acc[...]).astype(jnp.bfloat16)

    for copy in started:
        copy.wait_send()


def on_device(momentum):
    bf16, f32 = jnp.bfloat16, jnp.float32
    dma = pltpu.SemaphoreType.DMA
    return pl.pallas_call(
        kernel,
        out_shape=jax.ShapeDtypeStruct((B, W), bf16),
        in_specs=[pl.BlockSpec(memory_space=pltpu.VMEM)],
        out_specs=pl.BlockSpec(memory_space=pltpu.VMEM),
        scratch_shapes=[
            pltpu.VMEM((4, 4, PACK, 128), bf16),
            pltpu.VMEM((4, 4, B, B), f32),
            pltpu.VMEM((4, 4, H, B), bf16),
            pltpu.VMEM((4, 4, H, B), bf16),
            pltpu.VMEM((4, 3, H, B), bf16),
            pltpu.VMEM((4, 3, H, B), bf16),
            pltpu.VMEM((4, H, B), f32),
            pltpu.VMEM((3, H, B), bf16),
            pltpu.VMEM((3, H, B), bf16),
            pltpu.VMEM((4, 4, H, B), bf16),
            pltpu.VMEM((4, 2, 4, H, B), bf16),
            pltpu.VMEM((4, 2, 4, H, B), bf16),
            pltpu.VMEM((B, W), f32),
            dma((6, 4, 4)),
            dma((4, 4, 4)),
            dma((5, 4)),
            dma((5, 4)),
            dma((15, 4)),
            dma((9, 4)),
            dma((8, 4)),
            dma((5, 4)),
        ],
        compiler_params=pltpu.CompilerParams(
            collective_id=0, has_side_effects=True, vmem_limit_bytes=48 * 2**20
        ),
        cost_estimate=pl.CostEstimate(flops=4 * 10**9, bytes_accessed=2 * 10**7, transcendentals=0),
    )(momentum)


def solution(mesh):
    return jax.shard_map(
        on_device, mesh=mesh, in_specs=(P("row", "col"),), out_specs=P("row", "col"), check_vma=False
    )
```

time: 468 us -> 137 us (0.29)
  waiting for transfers between devices: 373 us -> 0 us
  Pallas kernels: 0 us -> 135 us
  blocking collectives: 65.1 us -> 0 us
  matrix products: 13.5 us -> 0 us
  between operations: 13.1 us -> 0.01 us
    all_gather x3 -> x0, waiting for transfers between devices: 223 us -> none  [the longest x1 149 us: on_device(): slab_panel = lax.all_gather(momentum, 'row', axis=0, tiled=True)]
    reduce_scatter x1 -> x0, waiting for transfers between devices: 149 us -> none  [on_device(): lax.psum_scatter(lax.dot_general(slab_piece, momentum, (((1,), (1,)), (()...]
    pallas_call x0 -> x1, Pallas kernels: none -> 135 us  [on_device(): pl.pallas_call(kernel, out_shape=jax.ShapeDtypeStruct((B, W), bf16), in_s...]
    all_gather x1 -> x0, blocking collectives: 65.1 us -> none  [on_device(): gram_cols = lax.all_gather(gram_tile, 'row', axis=0, tiled=True)]
    dot_general x3 -> x0, matrix products: 13.5 us -> none  [the longest x1 5.77 us: on_device(): lax.dot_general(slab_piece, momentum, (((1,), (1,)), ((), ())), preferred...]
  transfers between devices with their start and end apart: 4 -> 0, of which waited for: 4 -> 0; matrix products, arithmetic and copies ran while one was open for 0% -> 0% of each run, Pallas kernels for 0% -> 0%
where the time goes in v1:
time: 137 us
  Pallas kernels  135 us (99%)
  local copies, waits for them, and re-layouts  1.67 us (1%)
    pallas_call x1, Pallas kernels, on_device(): pl.pallas_call(kernel, out_shape=jax.ShapeDtypeStruct((B, W), bf16), in_s...  135 us

profile of v1, /device:TPU:1, one launch (start us, length us, event | category | flops | bytes accessed | tf_op | source)
XLA Modules:
  0.0 137.0 jit_solution(14703032266240828574)
XLA Ops:
  0.0 0.0 copy-start
  0.0 1.0 copy-done
  1.0 135.3 %shard_map.17 = bf16[224,576]{1,0:T(8,128)(2,1)S(1)} custom-call(bf16[224,576]{1,0:T(8,128)(2,1)S(1)} %copy-done), custom_call_target="tpu_custom_call" | custom-call | flops 4000000000 | bytes 20000000 | tf_op jit(solution)/shard_map/pallas_call | solution.py:333
  136.2 0.7 copy.3
Async XLA Ops:
  0.0 1.0 copy-start

commit v2 on v1

v2 whole, which is shorter than its diff:
```python
import jax
import jax.numpy as jnp
from jax import lax
from jax.experimental import pallas as pl
from jax.experimental.pallas import tpu as pltpu
from jax.sharding import PartitionSpec as P

NR = 3584
NC = 18432

coef_a = 3.4445
coef_b = -4.775
coef_c = 2.0315
factor = 0.2 * max(NR, NC) ** 0.5

MESH = pl.DeviceIdType.MESH

B = 224
H = 112
W = 576
TILES = 4
PACK = TILES * B + H
LOW = (0, 2 * B)
HIGH = (2 * B, 2 * B + H)
REST = (TILES * B, H)


def nt_dot(a, b):
    return lax.dot_general(a, b, (((1,), (1,)), ((), ())), preferred_element_type=jnp.float32)


def nn_dot(a, b):
    return lax.dot_general(a, b, (((1,), (0,)), ((), ())), preferred_element_type=jnp.float32)


def kernel(
    x_ref,
    o_ref,
    xs,
    part,
    send1,
    recv1,
    send2,
    recv2,
    sum2,
    send3,
    recv3,
    swap_send,
    swap_recv,
    flip_send,
    flip_recv,
    swap_sum,
    flip_sum,
    gr,
    gc,
    pr,
    acc,
    zsend,
    zrecv,
    xsend,
    xrecv,
    rsend,
    rrecv,
    tsend,
    trecv,
    gsend,
    grecv,
    psend,
    precv,
):
    row = lax.axis_index("row")
    col = lax.axis_index("col")
    x, zh = row // 4, row % 4
    y, zl, k = col // 8, (col // 2) % 4, col % 2
    sign = 1 + 2 * (zl % 2)

    def place(x_, zh_, y_, zl_, k_):
        return (x_ * 4 + zh_, y_ * 8 + zl_ * 2 + k_)

    def at(dx=0, dzh=0, dy=0, dzl=0, dk=0):
        return place((x + dx) % 4, (zh + dzh) % 4, (y + dy) % 4, (zl + dzl) % 4, (k + dk) % 2)

    def station(dz):
        return (zh + sign * dz) % 4

    started = []

    def send(src, dst, ssem, rsem, device):
        copy = pltpu.make_async_remote_copy(
            src_ref=src, dst_ref=dst, send_sem=ssem, recv_sem=rsem, device_id=device, device_id_type=MESH
        )
        copy.start()
        started.append(copy)

    def arrived(dst, rsem):
        pltpu.make_async_copy(dst, dst, rsem).wait()

    def rest(zp, xp):
        last = xs[zp, xp, pl.ds(TILES * B, H), :]
        return jnp.concatenate([last[:, :64], last[:, 64:]], axis=0)

    def tile_of(zp, xp, t):
        return xs[zp, xp, pl.ds(pl.multiple_of(t * B, 16), B), :]

    def unpack(zp, xp):
        return jnp.concatenate([tile_of(zp, xp, t) for t in range(TILES)] + [rest(zp, xp)], axis=1)

    for t in range(TILES):
        xs[zh, x, pl.ds(t * B, B), :] = x_ref[:, pl.ds(t * 128, 128)]
    xs[zh, x, pl.ds(TILES * B, H), :] = jnp.concatenate(
        [x_ref[pl.ds(0, H), pl.ds(TILES * 128, 64)], x_ref[pl.ds(H, H), pl.ds(TILES * 128, 64)]], axis=1
    )

    barrier = pltpu.get_barrier_semaphore()
    peers = [at(dx=d) for d in (1, 2, 3)] + [at(dzh=d) for d in (1, 2, 3)]
    peers += [at(dy=d) for d in (1, 2, 3)] + [at(dzl=d) for d in (1, 2, 3)] + [at(dk=1)]
    swap_peer = place(y, zh, x, zl, k)
    flip_peers = [place(x, zl, y, zh, n) for n in range(2)]
    for peer in peers:
        pl.semaphore_signal(barrier, 1, device_id=peer, device_id_type=MESH)

    @pl.when(x != y)
    def _():
        pl.semaphore_signal(barrier, 1, device_id=swap_peer, device_id_type=MESH)

    @pl.when(zh != zl)
    def _():
        for peer in flip_peers:
            pl.semaphore_signal(barrier, 1, device_id=peer, device_id_type=MESH)

    pl.semaphore_wait(barrier, len(peers) + jnp.where(x != y, 1, 0) + jnp.where(zh != zl, 2, 0))

    def rows(dz, dx, start, size):
        return xs.at[station(dz), (x + dx) % 4, pl.ds(start, size)]

    def zmove(sem, dz, start, size, hop, rsem):
        piece = rows(dz, 0, start, size)
        send(piece, piece, zsend.at[sem], rsem, at(dzh=sign * hop))

    def xmove(kind, dz, dx, part_, hop):
        piece = rows(dz, dx, *(LOW, HIGH)[part_])
        send(piece, piece, xsend.at[kind, dz, part_], xrecv.at[dz, (dx - hop) % 4, part_], at(dx=hop))

    def xwait(dz, dx, part_):
        arrived(rows(dz, dx, *(LOW, HIGH)[part_]), xrecv.at[dz, dx, part_])

    def x_spread(dz, part_):
        xmove(0, dz, 0, part_, 1)
        xmove(1, dz, 0, part_, 3)

    def x_forward(dz, part_):
        source, hop = ((3, 1), (1, 3))[part_]
        xwait(dz, source, part_)
        xmove(2, dz, source, part_, hop)

    def x_rest(dz):
        for part_, source in ((0, 1), (1, 3)):
            xwait(dz, source, part_)
            xwait(dz, 2, part_)

    def tile_rows(t):
        return pl.multiple_of(t * B, 16)

    def zwait(dz, t):
        arrived(rows(dz, 0, tile_rows(t), B), zrecv.at[dz, t])

    def zwait_rest(dz):
        arrived(rows(dz, 0, *REST), zrecv.at[dz, 4])

    half = zh // 2
    half_before = ((zh + 4 - sign) % 4) // 2
    half_after = ((zh + sign) % 4) // 2

    def gram(dz):
        zp = station(dz)

        def step(xp, carry):
            if dz == 0:
                left, right = unpack(zh, xp), unpack(zh, x)
                value = 0.5 * nt_dot(left, right)
            elif dz == 1:
                left, right = [jnp.concatenate([tile_of(*b, t) for t in (0, 1)], axis=1) for b in ((zh, xp), (zp, x))]
                value = nt_dot(left, right)
            elif dz == 3:
                left, right = [
                    jnp.concatenate([tile_of(*b, t) for t in (2, 3)] + [rest(*b)], axis=1) for b in ((zh, xp), (zp, x))
                ]
                value = nt_dot(left, right)
            else:
                left, right = [
                    jnp.concatenate([tile_of(*b, half), tile_of(*b, 2 + half)], axis=1) for b in ((zh, xp), (zp, x))
                ]
                value = nt_dot(left, right) + 0.5 * nt_dot(rest(zh, xp), rest(zp, x))
            part[dz, xp] = value
            send1[dz, xp] = part[dz, xp, pl.ds(pl.multiple_of((1 - k) * H, 16), H), :].astype(jnp.bfloat16)
            return carry

        lax.fori_loop(0, 4, step, 0)
        send(send1.at[dz], recv1.at[dz], rsend.at[0, dz], rrecv.at[0, dz], at(dk=1))

    def reduce_core(dz):
        arrived(recv1.at[dz], rrecv.at[0, dz])

        def both(xp):
            return part[dz, xp, pl.ds(pl.multiple_of(k * H, 16), H), :] + recv1[dz, xp].astype(jnp.float32)

        for dy in (2, 1, 3):
            send2[dz, dy - 1] = both((y + dy) % 4).astype(jnp.bfloat16)
            send(send2.at[dz, dy - 1], recv2.at[dz, dy - 1], rsend.at[dy, dz], rrecv.at[dy, dz], at(dy=dy))
        sum2[dz] = both(y)

    def sum3(dz):
        owner = station(dz)
        d = (owner + 4 - zl) % 4
        copy = pltpu.make_async_remote_copy(
            src_ref=send3.at[dz],
            dst_ref=recv3.at[d],
            send_sem=rsend.at[4, dz],
            recv_sem=rrecv.at[4, d],
            device_id=place(x, zh, y, owner, k),
            device_id_type=MESH,
        )
        return d, copy

    def reduce_y(dz):
        for dy in (1, 3, 2):
            arrived(recv2.at[dz, dy - 1], rrecv.at[dy, dz])
        total = sum2[dz]
        for dy in (1, 2, 3):
            total = total + recv2[dz, dy - 1].astype(jnp.float32)
        sum2[dz] = total
        send3[dz] = total.astype(jnp.bfloat16)
        d, copy = sum3(dz)

        @pl.when(d != 0)
        def _():
            copy.start()

    for t in (0, 1):
        zmove((0, t), 0, t * B, B, 3, zrecv.at[1, t])
        zmove((0, 2 + t), 0, (2 + t) * B, B, 1, zrecv.at[3, 2 + t])
        xmove(t, 0, 0, t, 1 + 2 * t)
    zmove((0, 4), 0, *REST, 1, zrecv.at[3, 4])
    for t in (0, 1):
        xmove(1 - t, 0, 0, t, 3 - 2 * t)
    x_forward(0, 0)
    x_forward(0, 1)
    zwait(1, half_before)
    zmove((2, 0), 1, tile_rows(half_before), B, 3, zrecv.at[2, half_before])
    zwait(3, 2 + half_after)
    zmove((2, 1), 3, tile_rows(2 + half_after), B, 1, zrecv.at[2, 2 + half_after])
    zwait_rest(3)
    zmove((2, 2), 3, *REST, 1, zrecv.at[2, 4])
    x_rest(0)
    gram(0)
    zwait(1, 1 - half_before)
    gram(1)
    x_spread(1, 0)
    zwait(3, 3 - half_after)
    gram(3)
    x_spread(3, 1)
    reduce_core(0)
    reduce_core(1)
    reduce_core(3)
    reduce_y(0)
    zwait(2, half)
    zwait(2, 2 + half)
    zwait_rest(2)
    gram(2)
    zmove((1, 0), 0, *HIGH, 3, zrecv.at[1, 2])
    zmove((1, 1), 0, *LOW, 1, zrecv.at[3, 0])
    zmove((3, 0), 1, tile_rows(1 - half_before), B, 3, zrecv.at[2, 1 - half_before])
    zmove((3, 1), 3, tile_rows(3 - half_after), B, 1, zrecv.at[2, 3 - half_after])
    reduce_y(1)
    reduce_y(3)
    x_forward(1, 0)
    x_forward(3, 1)
    reduce_core(2)
    reduce_y(2)

    total = sum2[(sign * (zl + 4 - zh)) % 4]
    for d in (1, 2, 3):
        arrived(recv3.at[d], rrecv.at[4, d])
        total = total + recv3[d].astype(jnp.float32)

    swap_send[...] = total.astype(jnp.bfloat16)
    flipped = total.T
    for n in range(2):
        flip_send[n] = flipped[n * H : (n + 1) * H, :].astype(jnp.bfloat16)
    swap_copy = pltpu.make_async_remote_copy(
        src_ref=swap_send,
        dst_ref=swap_recv,
        send_sem=tsend.at[0],
        recv_sem=trecv.at[0],
        device_id=swap_peer,
        device_id_type=MESH,
    )

    def flip_copy(n):
        return pltpu.make_async_remote_copy(
            src_ref=flip_send.at[n],
            dst_ref=flip_recv.at[k],
            send_sem=tsend.at[1 + n],
            recv_sem=trecv.at[1 + k],
            device_id=place(x, zl, y, zh, n),
            device_id_type=MESH,
        )

    @pl.when(x != y)
    def _():
        swap_copy.start()

    @pl.when(x == y)
    def _():
        swap_sum[...] = total

    flip_copy(1 - k).start()

    @pl.when(zh != zl)
    def _():
        flip_copy(k).start()

    @pl.when(zh == zl)
    def _():
        swap_send2 = jnp.where(k == 0, flipped[:H, :], flipped[H:, :])
        flip_sum[k] = swap_send2

    arrived(rows(1, 0, *HIGH), zrecv.at[1, 2])
    x_spread(1, 1)
    arrived(rows(3, 0, *LOW), zrecv.at[3, 0])
    x_spread(3, 0)

    @pl.when(x != y)
    def _():
        arrived(swap_recv, trecv.at[0])
        swap_sum[...] = swap_recv[...].astype(jnp.float32)

    @pl.when(zh != zl)
    def _():
        arrived(flip_recv.at[k], trecv.at[1 + k])
        flip_sum[k] = flip_recv[k].astype(jnp.float32)

    arrived(flip_recv.at[1 - k], trecv.at[2 - k])
    flip_sum[1 - k] = flip_recv[1 - k].astype(jnp.float32)
    tile = (swap_sum[...] + jnp.concatenate([flip_sum[0], flip_sum[1]], axis=1)).astype(jnp.bfloat16)

    gr[zl, y] = tile
    gc[zh, k, x] = tile

    def row_move(buf, ssem, rsem, dzl, hop_zl, hop_y):
        piece = buf((zl + dzl) % 4, y)
        kind = hop_zl if hop_zl else 3 + hop_y
        there = ((dzl - hop_zl) % 4, (0 - hop_y) % 4)
        send(piece, piece, ssem.at[kind, dzl], rsem.at[there[0], there[1]], at(dzl=hop_zl, dy=hop_y))

    def gr_at(zp, yp):
        return gr.at[zp, yp]

    def gc_move(dz, hop_z, hop_x):
        piece = gc.at[(zh + dz) % 4, k, x]
        kind = 7 + (hop_z if hop_z else 3 + hop_x)
        there = ((dz - hop_z) % 4, (0 - hop_x) % 4)
        send(piece, piece, gsend.at[kind, dz], grecv.at[4 + there[0], there[1]], at(dzh=hop_z, dx=hop_x))

    for d in (1, 3, 2):
        gc_move(0, d, 0)
        row_move(gr_at, gsend, grecv, 0, d, 0)
    for d in (1, 3, 2):
        gc_move(0, 0, d)
        row_move(gr_at, gsend, grecv, 0, 0, d)
    for n in (3, 1, 2):
        arrived(gr.at[(zl + n) % 4, y], grecv.at[n, 0])
        for d in (1, 3, 2):
            row_move(gr_at, gsend, grecv, n, 0, d)
    for n in (3, 1, 2):
        arrived(gc.at[(zh + n) % 4, k, x], grecv.at[4 + n, 0])
        for d in (1, 3, 2):
            gc_move(n, 0, d)
    for n in (0, 3, 1, 2):
        zp = (zh + n) % 4
        for d in (1, 3, 2):
            arrived(gc.at[zp, k, (x + d) % 4], grecv.at[4 + n, d])
        send(gc.at[zp, k], gc.at[zp, k], gsend.at[14, n], grecv.at[8, n], at(dk=1))
    for n in range(4):
        for d in (1, 3, 2):
            arrived(gr.at[(zl + n) % 4, (y + d) % 4], grecv.at[n, d])
    for n in range(4):
        zp = (zh + n) % 4
        arrived(gc.at[zp, 1 - k], grecv.at[8, n])

    square = jnp.zeros((H, B), jnp.float32)
    for zp in range(4):
        for xp in range(4):
            right = jnp.concatenate([gc[zp, 0, xp], gc[zp, 1, xp]], axis=0)
            square = square + nn_dot(gr[zp, xp], right)
    zwait(2, 1 - half)
    zwait(2, 3 - half)
    pr[zl, k, y] = (coef_b * gr[zl, y].astype(jnp.float32) + coef_c * square).astype(jnp.bfloat16)

    def pr_at(zp, yp):
        return pr.at[zp, k, yp]

    for d in (1, 3, 2):
        row_move(pr_at, psend, precv, 0, d, 0)
    for d in (1, 3, 2):
        row_move(pr_at, psend, precv, 0, 0, d)
    x_spread(2, 0)
    x_spread(2, 1)
    x_forward(1, 1)
    x_forward(3, 0)
    for n in (3, 1, 2):
        arrived(pr_at((zl + n) % 4, y), precv.at[n, 0])
        for d in (1, 3, 2):
            row_move(pr_at, psend, precv, n, 0, d)
    for n in (0, 3, 1, 2):
        zp = (zl + n) % 4
        for d in (1, 3, 2):
            arrived(pr_at(zp, (y + d) % 4), precv.at[n, d])
        send(pr.at[zp, k], pr.at[zp, k], psend.at[7, n], precv.at[4, n], at(dk=1))

    x_forward(2, 0)
    x_forward(2, 1)
    for dz in (1, 3, 2):
        x_rest(dz)

    for n, d in enumerate((0, 3, 1, 2)):
        zp = (zl + d) % 4
        arrived(pr.at[zp, 1 - k], precv.at[4, d])

        def step(xp, carry, zp=zp, first=n == 0):
            left = jnp.concatenate([pr[zp, 0, xp], pr[zp, 1, xp]], axis=0)
            acc[...] += nn_dot(left, unpack(zp, xp))
            return carry

        if n == 0:
            acc[...] = coef_a * x_ref[...].astype(jnp.float32)
        lax.fori_loop(0, 4, step, 0)
    o_ref[...] = (factor * acc[...]).astype(jnp.bfloat16)

    for copy in started:
        copy.wait_send()
    for dz in range(4):
        d, copy = sum3(dz)

        @pl.when(d != 0)
        def _(copy=copy):
            copy.wait_send()

    flip_copy(1 - k).wait_send()

    @pl.when(zh != zl)
    def _():
        flip_copy(k).wait_send()

    @pl.when(x != y)
    def _():
        swap_copy.wait_send()


def on_device(momentum):
    bf16, f32 = jnp.bfloat16, jnp.float32
    dma = pltpu.SemaphoreType.DMA
    return pl.pallas_call(
        kernel,
        out_shape=jax.ShapeDtypeStruct((B, W), bf16),
        in_specs=[pl.BlockSpec(memory_space=pltpu.VMEM)],
        out_specs=pl.BlockSpec(memory_space=pltpu.VMEM),
        scratch_shapes=[
            pltpu.VMEM((4, 4, PACK, 128), bf16),
            pltpu.VMEM((4, 4, B, B), f32),
            pltpu.VMEM((4, 4, H, B), bf16),
            pltpu.VMEM((4, 4, H, B), bf16),
            pltpu.VMEM((4, 3, H, B), bf16),
            pltpu.VMEM((4, 3, H, B), bf16),
            pltpu.VMEM((4, H, B), f32),
            pltpu.VMEM((4, H, B), bf16),
            pltpu.VMEM((4, H, B), bf16),
            pltpu.VMEM((H, B), bf16),
            pltpu.VMEM((H, B), bf16),
            pltpu.VMEM((2, H, H), bf16),
            pltpu.VMEM((2, H, H), bf16),
            pltpu.VMEM((H, B), f32),
            pltpu.VMEM((2, H, H), f32),
            pltpu.VMEM((4, 4, H, B), bf16),
            pltpu.VMEM((4, 2, 4, H, B), bf16),
            pltpu.VMEM((4, 2, 4, H, B), bf16),
            pltpu.VMEM((B, W), f32),
            dma((4, 5)),
            dma((4, 5)),
            dma((3, 4, 2)),
            dma((4, 4, 2)),
            dma((5, 4)),
            dma((5, 4)),
            dma((3,)),
            dma((3,)),
            dma((15, 4)),
            dma((9, 4)),
            dma((8, 4)),
            dma((5, 4)),
        ],
        compiler_params=pltpu.CompilerParams(
            collective_id=0, has_side_effects=True, vmem_limit_bytes=48 * 2**20
        ),
        cost_estimate=pl.CostEstimate(flops=4 * 10**9, bytes_accessed=2 * 10**7, transcendentals=0),
    )(momentum)


def solution(mesh):
    return jax.shard_map(
        on_device, mesh=mesh, in_specs=(P("row", "col"),), out_specs=P("row", "col"), check_vma=False
    )
```

time: 137 us -> 126 us (0.920)
  Pallas kernels: 135 us -> 125 us
    pallas_call x1, Pallas kernels: 135 us -> 125 us  [on_device(): pl.pallas_call(kernel, out_shape=jax.ShapeDtypeStruct((B, W), bf16), in_s...]
where the time goes in v2:
time: 126 us
  Pallas kernels  125 us (99%)
  local copies, waits for them, and re-layouts  1.67 us (1%)
    pallas_call x1, Pallas kernels, on_device(): pl.pallas_call(kernel, out_shape=jax.ShapeDtypeStruct((B, W), bf16), in_s...  125 us

profile of v2, /device:TPU:1, one launch (start us, length us, event | category | flops | bytes accessed | tf_op | source)
XLA Modules:
  0.0 126.3 jit_solution(18202661655440486166)
XLA Ops:
  0.0 0.0 copy-start
  0.0 1.0 copy-done
  1.0 124.6 %shard_map.17 = bf16[224,576]{1,0:T(8,128)(2,1)S(1)} custom-call(bf16[224,576]{1,0:T(8,128)(2,1)S(1)} %copy-done), custom_call_target="tpu_custom_call" | custom-call | flops 4000000000 | bytes 20000000 | tf_op jit(solution)/shard_map/pallas_call | solution.py:463
  125.6 0.7 copy.3
Async XLA Ops:
  0.0 1.0 copy-start

commit v3 on v2

--- a/solution.py
+++ b/solution.py
@@ -22,6 +22,8 @@
 PACK = TILES * B + H
 LOW = (0, 2 * B)
 HIGH = (2 * B, 2 * B + H)
+FIRST = (0, 64)
+SECOND = (64, 48)
 REST = (TILES * B, H)
 
 
@@ -34,8 +36,9 @@
 
 
 def kernel(
+    x_hbm,
+    o_ref,
     x_ref,
-    o_ref,
     xs,
     part,
     send1,
@@ -55,16 +58,21 @@
     gc,
     pr,
     acc,
+    load_sem,
     zsend,
     zrecv,
     xsend,
     xrecv,
+    x2send,
+    x2recv,
     rsend,
     rrecv,
     tsend,
     trecv,
     gsend,
     grecv,
+    csend,
+    crecv,
     psend,
     precv,
 ):
@@ -105,12 +113,8 @@
     def unpack(zp, xp):
         return jnp.concatenate([tile_of(zp, xp, t) for t in range(TILES)] + [rest(zp, xp)], axis=1)
 
-    for t in range(TILES):
-        xs[zh, x, pl.ds(t * B, B), :] = x_ref[:, pl.ds(t * 128, 128)]
-    xs[zh, x, pl.ds(TILES * B, H), :] = jnp.concatenate(
-        [x_ref[pl.ds(0, H), pl.ds(TILES * 128, 64)], x_ref[pl.ds(H, H), pl.ds(TILES * 128, 64)]], axis=1
-    )
-
+    load = pltpu.make_async_copy(x_hbm, x_ref, load_sem)
+    load.start()
     barrier = pltpu.get_barrier_semaphore()
     peers = [at(dx=d) for d in (1, 2, 3)] + [at(dzh=d) for d in (1, 2, 3)]
     peers += [at(dy=d) for d in (1, 2, 3)] + [at(dzl=d) for d in (1, 2, 3)] + [at(dk=1)]
@@ -128,6 +132,12 @@
         for peer in flip_peers:
             pl.semaphore_signal(barrier, 1, device_id=peer, device_id_type=MESH)
 
+    load.wait()
+    for t in range(TILES):
+        xs[zh, x, pl.ds(t * B, B), :] = x_ref[:, pl.ds(t * 128, 128)]
+    xs[zh, x, pl.ds(TILES * B, H), :] = jnp.concatenate(
+        [x_ref[pl.ds(0, H), pl.ds(TILES * 128, 64)], x_ref[pl.ds(H, H), pl.ds(TILES * 128, 64)]], axis=1
+    )
     pl.semaphore_wait(barrier, len(peers) + jnp.where(x != y, 1, 0) + jnp.where(zh != zl, 2, 0))
 
     def rows(dz, dx, start, size):
@@ -166,6 +176,29 @@
 
     def zwait_rest(dz):
         arrived(rows(dz, 0, *REST), zrecv.at[dz, 4])
+
+    def x2_rows(dx, t):
+        return rows(2, dx, *(REST if t is None else (tile_rows(t), B)))
+
+    def x2_move(kind, dx, t, hop):
+        piece, sem = x2_rows(dx, t), 4 if t is None else t
+        send(piece, piece, x2send.at[kind, sem], x2recv.at[(dx - hop) % 4, sem], at(dx=hop))
+
+    def x2_wait(dx, t):
+        arrived(x2_rows(dx, t), x2recv.at[dx, 4 if t is None else t])
+
+    def x2_spread(t):
+        x2_move(0, 0, t, 1)
+        x2_move(1, 0, t, 3)
+
+    def x2_forward(t, up):
+        source, hop = (3, 1) if up else (1, 3)
+        x2_wait(source, t)
+        x2_move(2, source, t, hop)
+
+    def x2_rest(t, up):
+        x2_wait(1 if up else 3, t)
+        x2_wait(2, t)
 
     half = zh // 2
     half_before = ((zh + 4 - sign) % 4) // 2
@@ -256,10 +289,10 @@
     zwait(1, 1 - half_before)
     gram(1)
     x_spread(1, 0)
+    reduce_core(0)
     zwait(3, 3 - half_after)
     gram(3)
     x_spread(3, 1)
-    reduce_core(0)
     reduce_core(1)
     reduce_core(3)
     reduce_y(0)
@@ -269,13 +302,15 @@
     gram(2)
     zmove((1, 0), 0, *HIGH, 3, zrecv.at[1, 2])
     zmove((1, 1), 0, *LOW, 1, zrecv.at[3, 0])
-    zmove((3, 0), 1, tile_rows(1 - half_before), B, 3, zrecv.at[2, 1 - half_before])
-    zmove((3, 1), 3, tile_rows(3 - half_after), B, 1, zrecv.at[2, 3 - half_after])
+    early = ((half, True), (2 + half, False), (None, True))
+    late = ((1 - half, True), (3 - half, False))
+    for t, up in early:
+        x2_spread(t)
     reduce_y(1)
+    reduce_core(2)
     reduce_y(3)
     x_forward(1, 0)
     x_forward(3, 1)
-    reduce_core(2)
     reduce_y(2)
 
     total = sum2[(sign * (zl + 4 - zh)) % 4]
@@ -325,6 +360,8 @@
         swap_send2 = jnp.where(k == 0, flipped[:H, :], flipped[H:, :])
         flip_sum[k] = swap_send2
 
+    for t, up in early:
+        x2_forward(t, up)
     arrived(rows(1, 0, *HIGH), zrecv.at[1, 2])
     x_spread(1, 1)
     arrived(rows(3, 0, *LOW), zrecv.at[3, 0])
@@ -347,94 +384,148 @@
     gr[zl, y] = tile
     gc[zh, k, x] = tile
 
-    def row_move(buf, ssem, rsem, dzl, hop_zl, hop_y):
-        piece = buf((zl + dzl) % 4, y)
-        kind = hop_zl if hop_zl else 3 + hop_y
-        there = ((dzl - hop_zl) % 4, (0 - hop_y) % 4)
-        send(piece, piece, ssem.at[kind, dzl], rsem.at[there[0], there[1]], at(dzl=hop_zl, dy=hop_y))
+    def cut(ref, piece):
+        return ref.at[pl.ds(*piece)]
+
+    def y_spread(buf, ssem, rsem, n):
+        piece = buf((zl + n) % 4, y)
+        for i, hop in enumerate((1, 3)):
+            send(piece, piece, ssem.at[n, i], rsem.at[n, 4 - hop], at(dy=hop))
+
+    def y_forward(buf, ssem, rsem, n):
+        for i, (source, hop, rows_) in enumerate(((3, 1, FIRST), (1, 3, SECOND))):
+            whole = buf((zl + n) % 4, (y + source) % 4)
+            arrived(whole, rsem.at[n, source])
+            send(cut(whole, rows_), cut(whole, rows_), ssem.at[n, 2 + i], rsem.at[n, 2 + 2 * i], at(dy=hop))
+
+    def y_rest(buf, rsem, n):
+        for i, rows_ in enumerate((FIRST, SECOND)):
+            arrived(cut(buf((zl + n) % 4, (y + 2) % 4), rows_), rsem.at[n, 2 + 2 * i])
+
+    def zl_spread(buf, ssem, rsem):
+        piece = buf(zl, y)
+        for d in (1, 3, 2):
+            send(piece, piece, ssem.at[d, 4], rsem.at[4 - d, 0], at(dzl=d))
+
+    def zl_wait(buf, rsem, n):
+        arrived(buf((zl + n) % 4, y), rsem.at[n, 0])
+
+    def x_gc_spread(n):
+        piece = gc.at[(zh + n) % 4, k, x]
+        for i, hop in enumerate((1, 3)):
+            send(piece, piece, csend.at[n, i], crecv.at[n, 4 - hop], at(dx=hop))
+
+    def x_gc_forward(n):
+        for i, (source, hop, rows_) in enumerate(((3, 1, FIRST), (1, 3, SECOND))):
+            whole = gc.at[(zh + n) % 4, k, (x + source) % 4]
+            arrived(whole, crecv.at[n, source])
+            send(cut(whole, rows_), cut(whole, rows_), csend.at[n, 2 + i], crecv.at[n, 2 + 2 * i], at(dx=hop))
+
+    def x_gc_core(n):
+        zp = (zh + n) % 4
+        for i, rows_ in enumerate((FIRST, SECOND)):
+            arrived(cut(gc.at[zp, k, (x + 2) % 4], rows_), crecv.at[n, 2 + 2 * i])
+        send(gc.at[zp, k], gc.at[zp, k], csend.at[n, 4], crecv.at[n, 6], at(dk=1))
+
+    def z_gc_spread():
+        piece = gc.at[zh, k, x]
+        for i, hop in enumerate((1, 3)):
+            send(piece, piece, csend.at[2 * i, 5], crecv.at[4 - hop, 0], at(dzh=hop))
+
+    def z_gc_forward():
+        for i, (source, hop, rows_) in enumerate(((3, 1, FIRST), (1, 3, SECOND))):
+            whole = gc.at[(zh + source) % 4, k, x]
+            arrived(whole, crecv.at[source, 0])
+            send(cut(whole, rows_), cut(whole, rows_), csend.at[1 + 2 * i, 5], crecv.at[2, 5 * i], at(dzh=hop))
+            x_gc_spread(source)
 
     def gr_at(zp, yp):
         return gr.at[zp, yp]
 
-    def gc_move(dz, hop_z, hop_x):
-        piece = gc.at[(zh + dz) % 4, k, x]
-        kind = 7 + (hop_z if hop_z else 3 + hop_x)
-        there = ((dz - hop_z) % 4, (0 - hop_x) % 4)
-        send(piece, piece, gsend.at[kind, dz], grecv.at[4 + there[0], there[1]], at(dzh=hop_z, dx=hop_x))
-
-    for d in (1, 3, 2):
-        gc_move(0, d, 0)
-        row_move(gr_at, gsend, grecv, 0, d, 0)
-    for d in (1, 3, 2):
-        gc_move(0, 0, d)
-        row_move(gr_at, gsend, grecv, 0, 0, d)
+    gsems = (gr_at, gsend, grecv)
+    z_gc_spread()
+    zl_spread(*gsems)
+    x_gc_spread(0)
+    y_spread(*gsems, 0)
+    y_forward(*gsems, 0)
+    x_gc_forward(0)
     for n in (3, 1, 2):
-        arrived(gr.at[(zl + n) % 4, y], grecv.at[n, 0])
-        for d in (1, 3, 2):
-            row_move(gr_at, gsend, grecv, n, 0, d)
+        zl_wait(gr_at, grecv, n)
+        y_spread(*gsems, n)
+    z_gc_forward()
+    x_gc_core(0)
+    x_forward(1, 1)
+    x_forward(3, 0)
     for n in (3, 1, 2):
-        arrived(gc.at[(zh + n) % 4, k, x], grecv.at[4 + n, 0])
-        for d in (1, 3, 2):
-            gc_move(n, 0, d)
+        y_forward(*gsems, n)
+    for i, rows_ in enumerate((FIRST, SECOND)):
+        arrived(cut(gc.at[(zh + 2) % 4, k, x], rows_), crecv.at[2, 5 * i])
+    x_gc_spread(2)
+    zmove((3, 0), 1, tile_rows(1 - half_before), B, 3, zrecv.at[2, 1 - half_before])
+    zmove((3, 1), 3, tile_rows(3 - half_after), B, 1, zrecv.at[2, 3 - half_after])
+    x_gc_forward(3)
+    x_gc_forward(1)
+    x_gc_core(3)
+    x_gc_core(1)
+    x_gc_forward(2)
+    for n in range(4):
+        y_rest(gr_at, grecv, n)
+    x_gc_core(2)
     for n in (0, 3, 1, 2):
         zp = (zh + n) % 4
-        for d in (1, 3, 2):
-            arrived(gc.at[zp, k, (x + d) % 4], grecv.at[4 + n, d])
-        send(gc.at[zp, k], gc.at[zp, k], gsend.at[14, n], grecv.at[8, n], at(dk=1))
-    for n in range(4):
-        for d in (1, 3, 2):
-            arrived(gr.at[(zl + n) % 4, (y + d) % 4], grecv.at[n, d])
-    for n in range(4):
-        zp = (zh + n) % 4
-        arrived(gc.at[zp, 1 - k], grecv.at[8, n])
+        arrived(gc.at[zp, 1 - k], crecv.at[n, 6])
 
     square = jnp.zeros((H, B), jnp.float32)
     for zp in range(4):
         for xp in range(4):
             right = jnp.concatenate([gc[zp, 0, xp], gc[zp, 1, xp]], axis=0)
             square = square + nn_dot(gr[zp, xp], right)
-    zwait(2, 1 - half)
-    zwait(2, 3 - half)
     pr[zl, k, y] = (coef_b * gr[zl, y].astype(jnp.float32) + coef_c * square).astype(jnp.bfloat16)
 
     def pr_at(zp, yp):
         return pr.at[zp, k, yp]
 
-    for d in (1, 3, 2):
-        row_move(pr_at, psend, precv, 0, d, 0)
-    for d in (1, 3, 2):
-        row_move(pr_at, psend, precv, 0, 0, d)
-    x_spread(2, 0)
-    x_spread(2, 1)
-    x_forward(1, 1)
-    x_forward(3, 0)
+    def p_core(n):
+        y_rest(pr_at, precv, n)
+        zp = (zl + n) % 4
+        send(pr.at[zp, k], pr.at[zp, k], psend.at[n, 5], precv.at[n, 5], at(dk=1))
+
+    def product(n):
+        zp = (zl + n) % 4
+        arrived(pr.at[zp, 1 - k], precv.at[n, 5])
+
+        def one(xp):
+            return nn_dot(jnp.concatenate([pr[zp, 0, xp], pr[zp, 1, xp]], axis=0), unpack(zp, xp))
+
+        acc[...] += (one(0) + one(1)) + (one(2) + one(3))
+
+    psems = (pr_at, psend, precv)
+    zl_spread(*psems)
+    y_spread(*psems, 0)
+    acc[...] = coef_a * x_ref[...].astype(jnp.float32)
+    y_forward(*psems, 0)
     for n in (3, 1, 2):
-        arrived(pr_at((zl + n) % 4, y), precv.at[n, 0])
-        for d in (1, 3, 2):
-            row_move(pr_at, psend, precv, n, 0, d)
-    for n in (0, 3, 1, 2):
-        zp = (zl + n) % 4
-        for d in (1, 3, 2):
-            arrived(pr_at(zp, (y + d) % 4), precv.at[n, d])
-        send(pr.at[zp, k], pr.at[zp, k], psend.at[7, n], precv.at[4, n], at(dk=1))
-
-    x_forward(2, 0)
-    x_forward(2, 1)
-    for dz in (1, 3, 2):
-        x_rest(dz)
-
-    for n, d in enumerate((0, 3, 1, 2)):
-        zp = (zl + d) % 4
-        arrived(pr.at[zp, 1 - k], precv.at[4, d])
-
-        def step(xp, carry, zp=zp, first=n == 0):
-            left = jnp.concatenate([pr[zp, 0, xp], pr[zp, 1, xp]], axis=0)
-            acc[...] += nn_dot(left, unpack(zp, xp))
-            return carry
-
-        if n == 0:
-            acc[...] = coef_a * x_ref[...].astype(jnp.float32)
-        lax.fori_loop(0, 4, step, 0)
+        zl_wait(pr_at, precv, n)
+        y_spread(*psems, n)
+    for t, up in late:
+        zwait(2, t)
+        x2_spread(t)
+    p_core(0)
+    for n in (3, 1, 2):
+        y_forward(*psems, n)
+    for t, up in late:
+        x2_forward(t, up)
+    x_rest(1)
+    x_rest(3)
+    p_core(3)
+    for t, up in early + late:
+        x2_rest(t, up)
+    product(0)
+    p_core(1)
+    product(3)
+    p_core(2)
+    product(1)
+    product(2)
     o_ref[...] = (factor * acc[...]).astype(jnp.bfloat16)
 
     for copy in started:
@@ -463,9 +554,10 @@
     return pl.pallas_call(
         kernel,
         out_shape=jax.ShapeDtypeStruct((B, W), bf16),
-        in_specs=[pl.BlockSpec(memory_space=pltpu.VMEM)],
+        in_specs=[pl.BlockSpec(memory_space=pl.ANY)],
         out_specs=pl.BlockSpec(memory_space=pltpu.VMEM),
         scratch_shapes=[
+            pltpu.VMEM((B, W), bf16),
             pltpu.VMEM((4, 4, PACK, 128), bf16),
             pltpu.VMEM((4, 4, B, B), f32),
             pltpu.VMEM((4, 4, H, B), bf16),
@@ -485,18 +577,23 @@
             pltpu.VMEM((4, 2, 4, H, B), bf16),
             pltpu.VMEM((4, 2, 4, H, B), bf16),
             pltpu.VMEM((B, W), f32),
+            dma,
             dma((4, 5)),
             dma((4, 5)),
             dma((3, 4, 2)),
             dma((4, 4, 2)),
+            dma((3, 5)),
+            dma((4, 5)),
             dma((5, 4)),
             dma((5, 4)),
             dma((3,)),
             dma((3,)),
-            dma((15, 4)),
-            dma((9, 4)),
-            dma((8, 4)),
-            dma((5, 4)),
+            dma((4, 5)),
+            dma((4, 5)),
+            dma((4, 6)),
+            dma((4, 7)),
+            dma((4, 6)),
+            dma((4, 6)),
         ],
         compiler_params=pltpu.CompilerParams(
             collective_id=0, has_side_effects=True, vmem_limit_bytes=48 * 2**20

time: 126 us -> 117 us (0.929)
  Pallas kernels: 125 us -> 115 us
    pallas_call x1, Pallas kernels: 125 us -> 115 us  [on_device(): pl.pallas_call(kernel, out_shape=jax.ShapeDtypeStruct((B, W), bf16), in_s...]
where the time goes in v3:
time: 117 us
  Pallas kernels  115 us (98%)
  local copies, waits for them, and re-layouts  1.67 us (1%)
    pallas_call x1, Pallas kernels, on_device(): pl.pallas_call(kernel, out_shape=jax.ShapeDtypeStruct((B, W), bf16), in_s...  115 us

profile of v3, /device:TPU:1, one launch (start us, length us, event | category | flops | bytes accessed | tf_op | source)
XLA Modules:
  0.0 116.5 jit_solution(1591091625902478979)
XLA Ops:
  0.0 0.0 copy-start
  0.0 1.0 copy-done
  1.0 114.9 %shard_map.17 = bf16[224,576]{1,0:T(8,128)(2,1)S(1)} custom-call(bf16[224,576]{1,0:T(8,128)(2,1)S(1)} %copy-done), custom_call_target="tpu_custom_call" | custom-call | flops 4000000000 | bytes 20000000 | tf_op jit(solution)/shard_map/pallas_call | solution.py:554
  115.8 0.7 copy.3
Async XLA Ops:
  0.0 1.0 copy-start

commit v4 on v3

--- a/solution.py
+++ b/solution.py
@@ -116,21 +116,12 @@
     load = pltpu.make_async_copy(x_hbm, x_ref, load_sem)
     load.start()
     barrier = pltpu.get_barrier_semaphore()
-    peers = [at(dx=d) for d in (1, 2, 3)] + [at(dzh=d) for d in (1, 2, 3)]
+    peers = [at(dx=d) for d in (1, 2, 3)] + [at(dzh=d) for d in (1, 3)]
     peers += [at(dy=d) for d in (1, 2, 3)] + [at(dzl=d) for d in (1, 2, 3)] + [at(dk=1)]
     swap_peer = place(y, zh, x, zl, k)
     flip_peers = [place(x, zl, y, zh, n) for n in range(2)]
     for peer in peers:
         pl.semaphore_signal(barrier, 1, device_id=peer, device_id_type=MESH)
-
-    @pl.when(x != y)
-    def _():
-        pl.semaphore_signal(barrier, 1, device_id=swap_peer, device_id_type=MESH)
-
-    @pl.when(zh != zl)
-    def _():
-        for peer in flip_peers:
-            pl.semaphore_signal(barrier, 1, device_id=peer, device_id_type=MESH)
 
     load.wait()
     for t in range(TILES):
@@ -138,7 +129,7 @@
     xs[zh, x, pl.ds(TILES * B, H), :] = jnp.concatenate(
         [x_ref[pl.ds(0, H), pl.ds(TILES * 128, 64)], x_ref[pl.ds(H, H), pl.ds(TILES * 128, 64)]], axis=1
     )
-    pl.semaphore_wait(barrier, len(peers) + jnp.where(x != y, 1, 0) + jnp.where(zh != zl, 2, 0))
+    pl.semaphore_wait(barrier, len(peers))
 
     def rows(dz, dx, start, size):
         return xs.at[station(dz), (x + dx) % 4, pl.ds(start, size)]
@@ -337,7 +328,7 @@
             dst_ref=flip_recv.at[k],
             send_sem=tsend.at[1 + n],
             recv_sem=trecv.at[1 + k],
-            device_id=place(x, zl, y, zh, n),
+            device_id=(flip_peers[0][0], y * 8 + zh * 2 + n),
             device_id_type=MESH,
         )
 
@@ -410,66 +401,51 @@
     def zl_wait(buf, rsem, n):
         arrived(buf((zl + n) % 4, y), rsem.at[n, 0])
 
-    def x_gc_spread(n):
+    def y_all(n):
+        piece = gr.at[(zl + n) % 4, y]
+        for d in (2, 1, 3):
+            send(piece, piece, gsend.at[n, d], grecv.at[n, 4 - d], at(dy=d))
+
+    def x_all(n):
         piece = gc.at[(zh + n) % 4, k, x]
-        for i, hop in enumerate((1, 3)):
-            send(piece, piece, csend.at[n, i], crecv.at[n, 4 - hop], at(dx=hop))
-
-    def x_gc_forward(n):
-        for i, (source, hop, rows_) in enumerate(((3, 1, FIRST), (1, 3, SECOND))):
-            whole = gc.at[(zh + n) % 4, k, (x + source) % 4]
-            arrived(whole, crecv.at[n, source])
-            send(cut(whole, rows_), cut(whole, rows_), csend.at[n, 2 + i], crecv.at[n, 2 + 2 * i], at(dx=hop))
+        for d in (2, 1, 3):
+            send(piece, piece, csend.at[n, d], crecv.at[n, 4 - d], at(dx=d))
 
     def x_gc_core(n):
         zp = (zh + n) % 4
-        for i, rows_ in enumerate((FIRST, SECOND)):
-            arrived(cut(gc.at[zp, k, (x + 2) % 4], rows_), crecv.at[n, 2 + 2 * i])
+        for d in (1, 3, 2):
+            arrived(gc.at[zp, k, (x + d) % 4], crecv.at[n, d])
         send(gc.at[zp, k], gc.at[zp, k], csend.at[n, 4], crecv.at[n, 6], at(dk=1))
-
-    def z_gc_spread():
-        piece = gc.at[zh, k, x]
-        for i, hop in enumerate((1, 3)):
-            send(piece, piece, csend.at[2 * i, 5], crecv.at[4 - hop, 0], at(dzh=hop))
-
-    def z_gc_forward():
-        for i, (source, hop, rows_) in enumerate(((3, 1, FIRST), (1, 3, SECOND))):
-            whole = gc.at[(zh + source) % 4, k, x]
-            arrived(whole, crecv.at[source, 0])
-            send(cut(whole, rows_), cut(whole, rows_), csend.at[1 + 2 * i, 5], crecv.at[2, 5 * i], at(dzh=hop))
-            x_gc_spread(source)
 
     def gr_at(zp, yp):
         return gr.at[zp, yp]
 
-    gsems = (gr_at, gsend, grecv)
-    z_gc_spread()
-    zl_spread(*gsems)
-    x_gc_spread(0)
-    y_spread(*gsems, 0)
-    y_forward(*gsems, 0)
-    x_gc_forward(0)
+    for i, hop in enumerate((1, 3)):
+        send(gc.at[zh, k, x], gc.at[zh, k, x], csend.at[2 * i, 5], crecv.at[4 - hop, 0], at(dzh=hop))
+    x_all(0)
+    y_all(0)
+    x_gc_core(0)
+    zl_spread(gr_at, gsend, grecv)
+    x_forward(1, 1)
+    x_forward(3, 0)
+    for i, (source, hop, rows_) in enumerate(((3, 1, FIRST), (1, 3, SECOND))):
+        whole = gc.at[(zh + source) % 4, k, x]
+        arrived(whole, crecv.at[source, 0])
+        send(cut(whole, rows_), cut(whole, rows_), csend.at[1 + 2 * i, 5], crecv.at[2, 5 * i], at(dzh=hop))
+        x_all(source)
     for n in (3, 1, 2):
         zl_wait(gr_at, grecv, n)
-        y_spread(*gsems, n)
-    z_gc_forward()
-    x_gc_core(0)
-    x_forward(1, 1)
-    x_forward(3, 0)
-    for n in (3, 1, 2):
-        y_forward(*gsems, n)
+        y_all(n)
+    x_gc_core(3)
+    x_gc_core(1)
     for i, rows_ in enumerate((FIRST, SECOND)):
         arrived(cut(gc.at[(zh + 2) % 4, k, x], rows_), crecv.at[2, 5 * i])
-    x_gc_spread(2)
+    x_all(2)
     zmove((3, 0), 1, tile_rows(1 - half_before), B, 3, zrecv.at[2, 1 - half_before])
     zmove((3, 1), 3, tile_rows(3 - half_after), B, 1, zrecv.at[2, 3 - half_after])
-    x_gc_forward(3)
-    x_gc_forward(1)
-    x_gc_core(3)
-    x_gc_core(1)
-    x_gc_forward(2)
     for n in range(4):
-        y_rest(gr_at, grecv, n)
+        for d in (1, 3, 2):
+            arrived(gr.at[(zl + n) % 4, (y + d) % 4], grecv.at[n, d])
     x_gc_core(2)
     for n in (0, 3, 1, 2):
         zp = (zh + n) % 4
@@ -554,7 +530,7 @@
     return pl.pallas_call(
         kernel,
         out_shape=jax.ShapeDtypeStruct((B, W), bf16),
-        in_specs=[pl.BlockSpec(memory_space=pl.ANY)],
+        in_specs=[pl.BlockSpec(memory_space=pltpu.HBM)],
         out_specs=pl.BlockSpec(memory_space=pltpu.VMEM),
         scratch_shapes=[
             pltpu.VMEM((B, W), bf16),
@@ -596,7 +572,7 @@
             dma((4, 6)),
         ],
         compiler_params=pltpu.CompilerParams(
-            collective_id=0, has_side_effects=True, vmem_limit_bytes=48 * 2**20
+            collective_id=0, has_side_effects=True, vmem_limit_bytes=60 * 2**20
         ),
         cost_estimate=pl.CostEstimate(flops=4 * 10**9, bytes_accessed=2 * 10**7, transcendentals=0),
     )(momentum)

time: 117 us -> 109 us (0.932)
  Pallas kernels: 115 us -> 108 us
    pallas_call x1, Pallas kernels: 115 us -> 108 us  [on_device(): pl.pallas_call(kernel, out_shape=jax.ShapeDtypeStruct((B, W), bf16), in_s...]
where the time goes in v4:
time: 109 us
  Pallas kernels  108 us (99%)
  local copies, waits for them, and re-layouts  1.69 us (2%)
    pallas_call x1, Pallas kernels, on_device(): pl.pallas_call(kernel, out_shape=jax.ShapeDtypeStruct((B, W), bf16), in_s...  108 us

profile of v4, /device:TPU:1, one launch (start us, length us, event | category | flops | bytes accessed | tf_op | source)
XLA Modules:
  0.0 109.3 jit_solution(82933384207762652)
XLA Ops:
  0.0 107.6 %shard_map.17 = bf16[224,576]{1,0:T(8,128)(2,1)} custom-call(bf16[224,576]{1,0:T(8,128)(2,1)} %x_hbm.1), custom_call_target="tpu_custom_call" | custom-call | flops 4000000000 | bytes 20000000 | tf_op jit(solution)/shard_map/pallas_call | solution.py:530
  107.6 1.7 %copy.3 = bf16[224,576]{1,0:T(8,128)(2,1)} copy(bf16[224,576]{1,0:T(8,128)(2,1)} %shard_map.17) | data formatting | bytes 516096

commit v5 on v4

--- a/solution.py
+++ b/solution.py
@@ -198,35 +198,36 @@
     def gram(dz):
         zp = station(dz)
 
-        def step(xp, carry):
-            if dz == 0:
-                left, right = unpack(zh, xp), unpack(zh, x)
-                value = 0.5 * nt_dot(left, right)
-            elif dz == 1:
-                left, right = [jnp.concatenate([tile_of(*b, t) for t in (0, 1)], axis=1) for b in ((zh, xp), (zp, x))]
-                value = nt_dot(left, right)
-            elif dz == 3:
-                left, right = [
-                    jnp.concatenate([tile_of(*b, t) for t in (2, 3)] + [rest(*b)], axis=1) for b in ((zh, xp), (zp, x))
-                ]
-                value = nt_dot(left, right)
-            else:
-                left, right = [
-                    jnp.concatenate([tile_of(*b, half), tile_of(*b, 2 + half)], axis=1) for b in ((zh, xp), (zp, x))
-                ]
-                value = nt_dot(left, right) + 0.5 * nt_dot(rest(zh, xp), rest(zp, x))
-            part[dz, xp] = value
-            send1[dz, xp] = part[dz, xp, pl.ds(pl.multiple_of((1 - k) * H, 16), H), :].astype(jnp.bfloat16)
-            return carry
-
-        lax.fori_loop(0, 4, step, 0)
+        def stack(piece):
+            return jnp.concatenate([piece(zh, xp) for xp in range(4)], axis=0)
+
+        def dot(pieces):
+            return nt_dot(
+                jnp.concatenate([stack(piece) for piece in pieces], axis=1),
+                jnp.concatenate([piece(zp, x) for piece in pieces], axis=1),
+            )
+
+        tiles = [lambda z_, x_, t=t: tile_of(z_, x_, t) for t in (0, 1, 2, 3, half, 2 + half)]
+        if dz == 0:
+            value = 0.5 * dot(tiles[:4] + [rest])
+        elif dz == 1:
+            value = dot(tiles[:2])
+        elif dz == 3:
+            value = dot(tiles[2:4] + [rest])
+        else:
+            value = dot(tiles[4:]) + 0.5 * dot([rest])
+        part[dz] = value
+        for xp in range(4):
+            mine = pl.multiple_of(xp * B + (1 - k) * H, 16)
+            send1[dz, xp] = part[dz, pl.ds(mine, H), :].astype(jnp.bfloat16)
         send(send1.at[dz], recv1.at[dz], rsend.at[0, dz], rrecv.at[0, dz], at(dk=1))
 
     def reduce_core(dz):
         arrived(recv1.at[dz], rrecv.at[0, dz])
 
         def both(xp):
-            return part[dz, xp, pl.ds(pl.multiple_of(k * H, 16), H), :] + recv1[dz, xp].astype(jnp.float32)
+            mine = pl.multiple_of(xp * B + k * H, 16)
+            return part[dz, pl.ds(mine, H), :] + recv1[dz, xp].astype(jnp.float32)
 
         for dy in (2, 1, 3):
             send2[dz, dy - 1] = both((y + dy) % 4).astype(jnp.bfloat16)
@@ -443,16 +444,15 @@
     x_all(2)
     zmove((3, 0), 1, tile_rows(1 - half_before), B, 3, zrecv.at[2, 1 - half_before])
     zmove((3, 1), 3, tile_rows(3 - half_after), B, 1, zrecv.at[2, 3 - half_after])
+    x_gc_core(2)
     for n in range(4):
         for d in (1, 3, 2):
             arrived(gr.at[(zl + n) % 4, (y + d) % 4], grecv.at[n, d])
-    x_gc_core(2)
+
+    square = jnp.zeros((H, B), jnp.float32)
     for n in (0, 3, 1, 2):
         zp = (zh + n) % 4
         arrived(gc.at[zp, 1 - k], crecv.at[n, 6])
-
-    square = jnp.zeros((H, B), jnp.float32)
-    for zp in range(4):
         for xp in range(4):
             right = jnp.concatenate([gc[zp, 0, xp], gc[zp, 1, xp]], axis=0)
             square = square + nn_dot(gr[zp, xp], right)
@@ -461,8 +461,17 @@
     def pr_at(zp, yp):
         return pr.at[zp, k, yp]
 
+    def p_all(n):
+        piece = pr_at((zl + n) % 4, y)
+        for d in (2, 1, 3):
+            send(piece, piece, psend.at[n, d], precv.at[n, 4 - d], at(dy=d))
+
     def p_core(n):
-        y_rest(pr_at, precv, n)
+        if n == 2:
+            for d in (1, 3, 2):
+                arrived(pr_at((zl + n) % 4, (y + d) % 4), precv.at[n, d])
+        else:
+            y_rest(pr_at, precv, n)
         zp = (zl + n) % 4
         send(pr.at[zp, k], pr.at[zp, k], psend.at[n, 5], precv.at[n, 5], at(dk=1))
 
@@ -480,14 +489,16 @@
     y_spread(*psems, 0)
     acc[...] = coef_a * x_ref[...].astype(jnp.float32)
     y_forward(*psems, 0)
-    for n in (3, 1, 2):
+    for n in (3, 1):
         zl_wait(pr_at, precv, n)
         y_spread(*psems, n)
+    zl_wait(pr_at, precv, 2)
+    p_all(2)
     for t, up in late:
         zwait(2, t)
         x2_spread(t)
     p_core(0)
-    for n in (3, 1, 2):
+    for n in (3, 1):
         y_forward(*psems, n)
     for t, up in late:
         x2_forward(t, up)
@@ -535,7 +546,7 @@
         scratch_shapes=[
             pltpu.VMEM((B, W), bf16),
             pltpu.VMEM((4, 4, PACK, 128), bf16),
-            pltpu.VMEM((4, 4, B, B), f32),
+            pltpu.VMEM((4, 4 * B, B), f32),
             pltpu.VMEM((4, 4, H, B), bf16),
             pltpu.VMEM((4, 4, H, B), bf16),
             pltpu.VMEM((4, 3, H, B), bf16),

time: 109 us -> 109 us (level)
  no operation moved by 1% of the time
where the time goes in v5:
time: 109 us
  Pallas kernels  107 us (98%)
  local copies, waits for them, and re-layouts  1.69 us (2%)
    pallas_call x1, Pallas kernels, on_device(): pl.pallas_call(kernel, out_shape=jax.ShapeDtypeStruct((B, W), bf16), in_s...  107 us

profile of v5, /device:TPU:1, one launch (start us, length us, event | category | flops | bytes accessed | tf_op | source)
XLA Modules:
  0.0 108.6 jit_solution(10009571279051039460)
XLA Ops:
  0.0 106.9 %shard_map.17 = bf16[224,576]{1,0:T(8,128)(2,1)} custom-call(bf16[224,576]{1,0:T(8,128)(2,1)} %x_hbm.1), custom_call_target="tpu_custom_call" | custom-call | flops 4000000000 | bytes 20000000 | tf_op jit(solution)/shard_map/pallas_call | solution.py:541
  106.9 1.7 %copy.3 = bf16[224,576]{1,0:T(8,128)(2,1)} copy(bf16[224,576]{1,0:T(8,128)(2,1)} %shard_map.17) | data formatting | bytes 516096

commit v6 on v5

--- a/solution.py
+++ b/solution.py
@@ -24,6 +24,8 @@
 HIGH = (2 * B, 2 * B + H)
 FIRST = (0, 64)
 SECOND = (64, 48)
+LATE_LOW = ((B, B), (0, B))
+LATE_HIGH = ((3 * B, B + H), (2 * B, B))
 REST = (TILES * B, H)
 
 
@@ -292,8 +294,8 @@
     zwait(2, 2 + half)
     zwait_rest(2)
     gram(2)
-    zmove((1, 0), 0, *HIGH, 3, zrecv.at[1, 2])
-    zmove((1, 1), 0, *LOW, 1, zrecv.at[3, 0])
+    zmove((1, 0), 0, *LATE_HIGH[0], 3, zrecv.at[1, 3])
+    zmove((1, 1), 0, *LATE_LOW[0], 1, zrecv.at[3, 1])
     early = ((half, True), (2 + half, False), (None, True))
     late = ((1 - half, True), (3 - half, False))
     for t, up in early:
@@ -352,12 +354,10 @@
         swap_send2 = jnp.where(k == 0, flipped[:H, :], flipped[H:, :])
         flip_sum[k] = swap_send2
 
+    zmove((1, 2), 0, *LATE_HIGH[1], 3, zrecv.at[1, 2])
+    zmove((1, 3), 0, *LATE_LOW[1], 1, zrecv.at[3, 0])
     for t, up in early:
         x2_forward(t, up)
-    arrived(rows(1, 0, *HIGH), zrecv.at[1, 2])
-    x_spread(1, 1)
-    arrived(rows(3, 0, *LOW), zrecv.at[3, 0])
-    x_spread(3, 0)
 
     @pl.when(x != y)
     def _():
@@ -412,10 +412,25 @@
         for d in (2, 1, 3):
             send(piece, piece, csend.at[n, d], crecv.at[n, 4 - d], at(dx=d))
 
+    def x_gc_spread(n):
+        piece = gc.at[(zh + n) % 4, k, x]
+        for i, hop in enumerate((1, 3)):
+            send(piece, piece, csend.at[n, i], crecv.at[n, 4 - hop], at(dx=hop))
+
+    def x_gc_forward(n):
+        for i, (source, hop, rows_) in enumerate(((3, 1, FIRST), (1, 3, SECOND))):
+            whole = gc.at[(zh + n) % 4, k, (x + source) % 4]
+            arrived(whole, crecv.at[n, source])
+            send(cut(whole, rows_), cut(whole, rows_), csend.at[n, 2 + i], crecv.at[n, 2 + 2 * i], at(dx=hop))
+
     def x_gc_core(n):
         zp = (zh + n) % 4
-        for d in (1, 3, 2):
-            arrived(gc.at[zp, k, (x + d) % 4], crecv.at[n, d])
+        if n % 2:
+            for i, rows_ in enumerate((FIRST, SECOND)):
+                arrived(cut(gc.at[zp, k, (x + 2) % 4], rows_), crecv.at[n, 2 + 2 * i])
+        else:
+            for d in (1, 3, 2):
+                arrived(gc.at[zp, k, (x + d) % 4], crecv.at[n, d])
         send(gc.at[zp, k], gc.at[zp, k], csend.at[n, 4], crecv.at[n, 6], at(dk=1))
 
     def gr_at(zp, yp):
@@ -427,23 +442,27 @@
     y_all(0)
     x_gc_core(0)
     zl_spread(gr_at, gsend, grecv)
-    x_forward(1, 1)
-    x_forward(3, 0)
     for i, (source, hop, rows_) in enumerate(((3, 1, FIRST), (1, 3, SECOND))):
         whole = gc.at[(zh + source) % 4, k, x]
         arrived(whole, crecv.at[source, 0])
         send(cut(whole, rows_), cut(whole, rows_), csend.at[1 + 2 * i, 5], crecv.at[2, 5 * i], at(dzh=hop))
-        x_all(source)
+        x_gc_spread(source)
     for n in (3, 1, 2):
         zl_wait(gr_at, grecv, n)
         y_all(n)
-    x_gc_core(3)
-    x_gc_core(1)
+    x_gc_forward(3)
+    x_gc_forward(1)
     for i, rows_ in enumerate((FIRST, SECOND)):
         arrived(cut(gc.at[(zh + 2) % 4, k, x], rows_), crecv.at[2, 5 * i])
     x_all(2)
     zmove((3, 0), 1, tile_rows(1 - half_before), B, 3, zrecv.at[2, 1 - half_before])
     zmove((3, 1), 3, tile_rows(3 - half_after), B, 1, zrecv.at[2, 3 - half_after])
+    for dz, part_, pieces in ((1, 1, LATE_HIGH), (3, 0, LATE_LOW)):
+        for n, piece in enumerate(pieces):
+            arrived(rows(dz, 0, *piece), zrecv.at[dz, (1 - n) + 2 * part_])
+        x_spread(dz, part_)
+    x_gc_core(3)
+    x_gc_core(1)
     x_gc_core(2)
     for n in range(4):
         for d in (1, 3, 2):
@@ -494,6 +513,8 @@
         y_spread(*psems, n)
     zl_wait(pr_at, precv, 2)
     p_all(2)
+    x_forward(1, 1)
+    x_forward(3, 0)
     for t, up in late:
         zwait(2, t)
         x2_spread(t)

time: 109 us -> 112 us (1.028)
  Pallas kernels: 107 us -> 109 us
    pallas_call x1, Pallas kernels: 107 us -> 109 us  [on_device(): pl.pallas_call(kernel, out_shape=jax.ShapeDtypeStruct((B, W), bf16), in_s...]
where the time goes in v6:
time: 112 us; the launch traced here: 111 us
  Pallas kernels  109 us (97%)
  local copies, waits for them, and re-layouts  1.69 us (2%)
    pallas_call x1, Pallas kernels, on_device(): pl.pallas_call(kernel, out_shape=jax.ShapeDtypeStruct((B, W), bf16), in_s...  109 us

profile of v6, /device:TPU:1, one launch (start us, length us, event | category | flops | bytes accessed | tf_op | source)
XLA Modules:
  0.0 110.6 jit_solution(17718617531918211183)
XLA Ops:
  0.0 108.8 %shard_map.17 = bf16[224,576]{1,0:T(8,128)(2,1)} custom-call(bf16[224,576]{1,0:T(8,128)(2,1)} %x_hbm.1), custom_call_target="tpu_custom_call" | custom-call | flops 4000000000 | bytes 20000000 | tf_op jit(solution)/shard_map/pallas_call | solution.py:562
  108.9 1.7 %copy.3 = bf16[224,576]{1,0:T(8,128)(2,1)} copy(bf16[224,576]{1,0:T(8,128)(2,1)} %shard_map.17) | data formatting | bytes 516096

commit v7 on v5

--- a/solution.py
+++ b/solution.py
@@ -379,21 +379,6 @@
     def cut(ref, piece):
         return ref.at[pl.ds(*piece)]
 
-    def y_spread(buf, ssem, rsem, n):
-        piece = buf((zl + n) % 4, y)
-        for i, hop in enumerate((1, 3)):
-            send(piece, piece, ssem.at[n, i], rsem.at[n, 4 - hop], at(dy=hop))
-
-    def y_forward(buf, ssem, rsem, n):
-        for i, (source, hop, rows_) in enumerate(((3, 1, FIRST), (1, 3, SECOND))):
-            whole = buf((zl + n) % 4, (y + source) % 4)
-            arrived(whole, rsem.at[n, source])
-            send(cut(whole, rows_), cut(whole, rows_), ssem.at[n, 2 + i], rsem.at[n, 2 + 2 * i], at(dy=hop))
-
-    def y_rest(buf, rsem, n):
-        for i, rows_ in enumerate((FIRST, SECOND)):
-            arrived(cut(buf((zl + n) % 4, (y + 2) % 4), rows_), rsem.at[n, 2 + 2 * i])
-
     def zl_spread(buf, ssem, rsem):
         piece = buf(zl, y)
         for d in (1, 3, 2):
@@ -467,11 +452,8 @@
             send(piece, piece, psend.at[n, d], precv.at[n, 4 - d], at(dy=d))
 
     def p_core(n):
-        if n == 2:
-            for d in (1, 3, 2):
-                arrived(pr_at((zl + n) % 4, (y + d) % 4), precv.at[n, d])
-        else:
-            y_rest(pr_at, precv, n)
+        for d in (1, 3, 2):
+            arrived(pr_at((zl + n) % 4, (y + d) % 4), precv.at[n, d])
         zp = (zl + n) % 4
         send(pr.at[zp, k], pr.at[zp, k], psend.at[n, 5], precv.at[n, 5], at(dk=1))
 
@@ -484,22 +466,16 @@
 
         acc[...] += (one(0) + one(1)) + (one(2) + one(3))
 
-    psems = (pr_at, psend, precv)
-    zl_spread(*psems)
-    y_spread(*psems, 0)
+    zl_spread(pr_at, psend, precv)
+    p_all(0)
     acc[...] = coef_a * x_ref[...].astype(jnp.float32)
-    y_forward(*psems, 0)
-    for n in (3, 1):
+    for n in (3, 1, 2):
         zl_wait(pr_at, precv, n)
-        y_spread(*psems, n)
-    zl_wait(pr_at, precv, 2)
-    p_all(2)
+        p_all(n)
     for t, up in late:
         zwait(2, t)
         x2_spread(t)
     p_core(0)
-    for n in (3, 1):
-        y_forward(*psems, n)
     for t, up in late:
         x2_forward(t, up)
     x_rest(1)

time: 109 us -> 109 us (level)
  no operation moved by 1% of the time
where the time goes in v7:
time: 109 us
  Pallas kernels  107 us (98%)
  local copies, waits for them, and re-layouts  1.69 us (2%)
    pallas_call x1, Pallas kernels, on_device(): pl.pallas_call(kernel, out_shape=jax.ShapeDtypeStruct((B, W), bf16), in_s...  107 us

profile of v7, /device:TPU:1, one launch (start us, length us, event | category | flops | bytes accessed | tf_op | source)
XLA Modules:
  0.0 108.6 jit_solution(2480059380438138120)
XLA Ops:
  0.0 106.9 %shard_map.17 = bf16[224,576]{1,0:T(8,128)(2,1)} custom-call(bf16[224,576]{1,0:T(8,128)(2,1)} %x_hbm.1), custom_call_target="tpu_custom_call" | custom-call | flops 4000000000 | bytes 20000000 | tf_op jit(solution)/shard_map/pallas_call | solution.py:517
  106.9 1.7 %copy.3 = bf16[224,576]{1,0:T(8,128)(2,1)} copy(bf16[224,576]{1,0:T(8,128)(2,1)} %shard_map.17) | data formatting | bytes 516096

commit v8 on v7

--- a/solution.py
+++ b/solution.py
@@ -481,10 +481,10 @@
     x_rest(1)
     x_rest(3)
     p_core(3)
+    p_core(1)
     for t, up in early + late:
         x2_rest(t, up)
     product(0)
-    p_core(1)
     product(3)
     p_core(2)
     product(1)

time: 109 us -> 109 us (level)
  no operation moved by 1% of the time
where the time goes in v8:
time: 109 us
  Pallas kernels  107 us (98%)
  local copies, waits for them, and re-layouts  1.69 us (2%)
    pallas_call x1, Pallas kernels, on_device(): pl.pallas_call(kernel, out_shape=jax.ShapeDtypeStruct((B, W), bf16), in_s...  107 us

profile of v8, /device:TPU:1, one launch (start us, length us, event | category | flops | bytes accessed | tf_op | source)
XLA Modules:
  0.0 108.6 jit_solution(11702315542034656557)
XLA Ops:
  0.0 106.9 %shard_map.17 = bf16[224,576]{1,0:T(8,128)(2,1)} custom-call(bf16[224,576]{1,0:T(8,128)(2,1)} %x_hbm.1), custom_call_target="tpu_custom_call" | custom-call | flops 4000000000 | bytes 20000000 | tf_op jit(solution)/shard_map/pallas_call | solution.py:517
  106.9 1.7 %copy.3 = bf16[224,576]{1,0:T(8,128)(2,1)} copy(bf16[224,576]{1,0:T(8,128)(2,1)} %shard_map.17) | data formatting | bytes 516096

commit v9 on v8

--- a/solution.py
+++ b/solution.py
@@ -468,13 +468,13 @@
 
     zl_spread(pr_at, psend, precv)
     p_all(0)
+    for t, up in late:
+        zwait(2, t)
+        x2_spread(t)
     acc[...] = coef_a * x_ref[...].astype(jnp.float32)
     for n in (3, 1, 2):
         zl_wait(pr_at, precv, n)
         p_all(n)
-    for t, up in late:
-        zwait(2, t)
-        x2_spread(t)
     p_core(0)
     for t, up in late:
         x2_forward(t, up)

time: 109 us -> 105 us (0.963)
  Pallas kernels: 107 us -> 103 us
    pallas_call x1, Pallas kernels: 107 us -> 103 us  [on_device(): pl.pallas_call(kernel, out_shape=jax.ShapeDtypeStruct((B, W), bf16), in_s...]
where the time goes in v9:
time: 105 us
  Pallas kernels  103 us (98%)
  local copies, waits for them, and re-layouts  1.69 us (2%)
    pallas_call x1, Pallas kernels, on_device(): pl.pallas_call(kernel, out_shape=jax.ShapeDtypeStruct((B, W), bf16), in_s...  103 us

profile of v9, /device:TPU:1, one launch (start us, length us, event | category | flops | bytes accessed | tf_op | source)
XLA Modules:
  0.0 105.0 jit_solution(17486503962026706505)
XLA Ops:
  0.0 103.3 %shard_map.17 = bf16[224,576]{1,0:T(8,128)(2,1)} custom-call(bf16[224,576]{1,0:T(8,128)(2,1)} %x_hbm.1), custom_call_target="tpu_custom_call" | custom-call | flops 4000000000 | bytes 20000000 | tf_op jit(solution)/shard_map/pallas_call | solution.py:517
  103.3 1.7 %copy.3 = bf16[224,576]{1,0:T(8,128)(2,1)} copy(bf16[224,576]{1,0:T(8,128)(2,1)} %shard_map.17) | data formatting | bytes 516096

commit v10 on v9

--- a/solution.py
+++ b/solution.py
@@ -485,8 +485,8 @@
     for t, up in early + late:
         x2_rest(t, up)
     product(0)
+    p_core(2)
     product(3)
-    p_core(2)
     product(1)
     product(2)
     o_ref[...] = (factor * acc[...]).astype(jnp.bfloat16)

time: 105 us -> 105 us (level)
  no operation moved by 1% of the time
where the time goes in v10:
time: 105 us
  Pallas kernels  103 us (98%)
  local copies, waits for them, and re-layouts  1.69 us (2%)
    pallas_call x1, Pallas kernels, on_device(): pl.pallas_call(kernel, out_shape=jax.ShapeDtypeStruct((B, W), bf16), in_s...  103 us

profile of v10, /device:TPU:1, one launch (start us, length us, event | category | flops | bytes accessed | tf_op | source)
XLA Modules:
  0.0 104.6 jit_solution(7190626032245962479)
XLA Ops:
  0.0 102.9 %shard_map.17 = bf16[224,576]{1,0:T(8,128)(2,1)} custom-call(bf16[224,576]{1,0:T(8,128)(2,1)} %x_hbm.1), custom_call_target="tpu_custom_call" | custom-call | flops 4000000000 | bytes 20000000 | tf_op jit(solution)/shard_map/pallas_call | solution.py:517
  102.9 1.7 %copy.3 = bf16[224,576]{1,0:T(8,128)(2,1)} copy(bf16[224,576]{1,0:T(8,128)(2,1)} %shard_map.17) | data formatting | bytes 516096
